TPU v7x, 32 devices: a whole 2x2x4 slice. The times are simulated.
32 devices in a mesh: wave: 8 (over z, y), lev: 4 (over x, core).
Axes of the slice: x: 2, y: 2, z: 4, core: 2. Of those that a mesh axis runs over, the one named last changes fastest.
Arguments:
- spectral: bfloat16 [1280, 256, 1280], P('wave', 'lev'), may hold values from -6 to 6
- legendre: bfloat16 [1280, 32, 1280], P('wave'), may hold values from -0.0034179688 to 0.0034179688
- wave_map: int32 [1280], replicated, may hold values from 0 to 1279, each once
- row_points: int32 [32], replicated, may hold values from 20 to 5136, as said below
- brackets: int32 [4], replicated, may hold values from 0 to 14, as said below
- lev_weight: float32 [4], replicated, may hold values from 0.05 to 0.95
- climatology: float32 [4, 64, 5248], P('lev', 'wave'), may hold values from 0.1 to 1
Outputs:
- anomaly: float32 [4, 64, 5248], P('lev', 'wave')
Inputs may be any that keep to these rules, and one draw needn't show every extreme that they name: `wave_map`: each wavenumber once. `row_points`: each is 20 + 4 i for a whole number i below 1280; some row has 5136 points. `brackets`: pressure level p has its lower bracket level among the 4 model levels of band p (levels b * 4 to b * 4 + 3 for band b); some pressure level outside the last band takes the last level of its band; the last pressure level takes 16 - 2.
All inputs are finite; a program needn't handle non-finite values.
Results may differ from a plain program's by a relative error of at most 0.0003.
Values sent between devices are 32-bit elements; how exact they have to be, the bound alone decides.
No kernel may reach another device: no remote copies, remote signals or barrier semaphores. Data moves between devices by JAX's collectives and lax.ppermute only.
A program may use at most 256 MiB of HBM per device.

v0:
```python
import functools
import math

import jax
import jax.numpy as jnp
import numpy as np
from jax import lax
from jax.experimental import pallas as pl
from jax.experimental.pallas import tpu as pltpu
from jax.sharding import PartitionSpec as P

M = 1280
NT = 1280
LEV_DEV = 4
STEPS = 4
FIELDS = 2
ROWPAD = 5248

FS = FIELDS * STEPS
PART = 2 * FS
SQ = 8
DEPTH = 3
HALF_M = M // 2
KPTS = 672
KPAD = 768
KBLK = 256
TABLE_STEPS = 7
TABLE_CUTS = 3
BUF = 1536
MIB = 1024 * 1024
F32 = jnp.float32
BF16 = jnp.bfloat16


def iota(shape, dim):
    return lax.broadcasted_iota(jnp.int32, shape, dim)


def legendre_kernel(
    first_group, count, wave_map, brackets, weight_ref, spec_hbm, leg_hbm, own_ref, prev_ref, between_ref,
    low_buf, up_buf, first_buf, leg_buf, own_rows, prev_rows, sems,
):
    groups = spec_hbm.shape[1]
    slots = SQ * groups
    step_slots = low_buf.shape[2]
    steps = count // step_slots
    half = leg_hbm.shape[2]
    wave = lax.axis_index("wave")
    lev = lax.axis_index("lev")
    lower = brackets[lev] - lev * LEV_DEV
    has_upper = lower < LEV_DEV - 1
    w = weight_ref[lev]
    upper_w = jnp.where(has_upper, 1.0 - w, 0.0)
    before = jnp.maximum(lev - 1, 0)
    crosses = (lev > 0) & (brackets[before] == lev * LEV_DEV - 1)
    first_w = jnp.where(crosses, 1.0 - weight_ref[before], 0.0)
    degree = iota((16, NT), 1).astype(jnp.int16)
    sign = (1 - 2 * (iota((16, NT), 1) % 2)).astype(F32).astype(BF16)
    lane_group = iota((1, 2 * SQ * PART), 1) % 64 // PART
    left = iota((1, SQ * PART), 1) < 64
    south = iota((2 * half, 1), 0) >= half

    def columns_copy(step, level, buf, kind):
        slot = step % DEPTH
        rows = pl.ds(pl.multiple_of(level * PART, PART), PART)
        src = spec_hbm.at[:, pl.ds(first_group + step * step_slots, step_slots), rows, :]
        return pltpu.make_async_copy(src, buf.at[slot], sems.at[slot, kind])

    def values_copy(step):
        slot = step % DEPTH
        src = leg_hbm.at[:, pl.ds(first_group + step * step_slots, step_slots)]
        return pltpu.make_async_copy(src, leg_buf.at[slot], sems.at[slot, 3])

    upper = jnp.minimum(lower + 1, LEV_DEV - 1)

    def copies(step):
        return [
            values_copy(step),
            columns_copy(step, lower, low_buf, 0),
            columns_copy(step, upper, up_buf, 1),
            columns_copy(step, 0, first_buf, 2),
        ]

    def fetch(step):
        for copy in copies(step):
            copy.start()

    for step in range(DEPTH - 1):
        fetch(step)
    between = jnp.int32(0)
    for p in range(1, brackets.shape[0] - 1, 2):
        between = between | (brackets[p] == (p + 1) * LEV_DEV - 1).astype(jnp.int32)
    between_ref[0] = between

    def step_body(step, carry):
        slot = step % DEPTH
        for copy in copies(step):
            copy.wait()

        @pl.when(step + DEPTH - 1 < steps)
        def _():
            fetch(step + DEPTH - 1)

        for b in range(step_slots):
            owns, firsts = [], []
            for quad in range(2):
                values, factors = [], []
                for sq in range(4 * quad, 4 * quad + 4):
                    m = wave_map[wave * slots + sq * groups + first_group + step * step_slots + b]
                    kept = degree >= m.astype(jnp.int16)
                    plain = [jnp.where(kept, leg_buf[slot, sq, b, i : i + 16, :], 0) for i in range(0, half, 16)]
                    values += plain + [x * sign for x in plain]
                    factors.append(jnp.where(south, (1 - 2 * (m % 2)).astype(F32), 1.0))
                bufs = (low_buf, up_buf, first_buf) if quad == 0 else (up_buf, low_buf, first_buf)
                columns = [buf[slot, sq, b] for buf in bufs for sq in range(4 * quad, 4 * quad + 4)]
                sums = nt_dot(jnp.concatenate(values, axis=0), jnp.concatenate(columns, axis=0))
                kept_sums = sums[: 2 * half] * factors[0]
                for a in range(1, 4):
                    block = sums[2 * half * a : 2 * half * (a + 1)] * factors[a]
                    kept_sums = jnp.where(lane_group[:, :192] == a, block, kept_sums)
                both = kept_sums[:, :128]
                other = pltpu.roll(both, 64, 1)
                owns.append(both * w + other * upper_w)
                firsts.append(jnp.concatenate([kept_sums[:, 128:]] * 2, axis=1))
            at = pl.multiple_of((step * step_slots + b) * 2 * half, 2 * half)
            own_rows[pl.ds(at, 2 * half), :] = jnp.where(left, owns[0], owns[1])
            prev_rows[pl.ds(at, 2 * half), :] = jnp.where(left, firsts[0], firsts[1]) * first_w
        return carry

    lax.fori_loop(0, steps, step_body, 0)
    rows = 2 * half
    for rows_ref, ref in ((own_rows, own_ref), (prev_rows, prev_ref)):
        rows_dev = ref.shape[1] // count
        for r in range(rows):
            at = (r % rows_dev) * count
            ref[r // rows_dev, at : at + count, :] = rows_ref[pl.ds(r, count, stride=rows), :]


def legendre_sums(first_group, count, spectral, legendre, wave_map, brackets, lev_weight):
    slots, cols, _ = spectral.shape
    half = legendre.shape[1]
    groups = slots // SQ
    step_slots = 4 if count % 4 == 0 else 2
    spec = spectral.reshape(SQ, groups, cols, NT)
    leg = legendre.reshape(SQ, groups, half, NT)
    devices = lax.axis_size("wave") * lax.axis_size("lev")
    out = pltpu.VMEM((devices, 2 * half // devices * count, SQ * PART), F32)
    smem = pl.BlockSpec(memory_space=pltpu.SMEM)
    vmem = pl.BlockSpec(memory_space=pltpu.VMEM)
    anywhere = pl.BlockSpec(memory_space=pltpu.HBM)
    return pl.pallas_call(
        functools.partial(legendre_kernel, first_group, count),
        out_shape=[out, out, jax.ShapeDtypeStruct((1,), jnp.int32)],
        in_specs=[smem, smem, smem, anywhere, anywhere],
        out_specs=[vmem, vmem, smem],
        scratch_shapes=[pltpu.VMEM((DEPTH, SQ, step_slots, PART, NT), BF16)] * 3
        + [pltpu.VMEM((DEPTH, SQ, step_slots, half, NT), BF16)]
        + [pltpu.VMEM((count * 2 * half, SQ * PART), F32)] * 2
        + [pltpu.SemaphoreType.DMA((DEPTH, 4))],
        compiler_params=pltpu.CompilerParams(vmem_limit_bytes=48 * MIB),
        cost_estimate=pl.CostEstimate(
            flops=2 * SQ * count * 2 * half * 48 * NT, bytes_accessed=SQ * count * NT * 2 * (48 + half), transcendentals=0
        ),
        name="legendre_sums",
    )(
        *[pltpu.with_memory_space_constraint(x, pltpu.HBM) for x in (wave_map, brackets, lev_weight, spec, leg)]
    )


def unit_circle(product, points, inverse):
    big = 12582912.0
    turn = (product * inverse + big) - big
    x = (product - turn * points) * (math.pi * inverse)
    x2 = x * x
    sine = 0.0
    cosine = 0.0
    for power in (11, 9, 7, 5, 3, 1):
        sine = sine * x2 + (-1) ** (power // 2) / math.factorial(power)
    for power in (12, 10, 8, 6, 4, 2, 0):
        cosine = cosine * x2 + (-1) ** (power // 2) / math.factorial(power)
    sine = sine * x
    twice = sine + sine
    return 1.0 - twice * sine, twice * cosine


def own_points(points_ref, r2):
    wave = lax.axis_index("wave")
    lev = lax.axis_index("lev")
    row = 2 * (wave * lax.axis_size("lev") + lev) + r2
    return points_ref[row % points_ref.shape[0]]


def table_kernel(points_ref, hi_ref, lo_ref):
    r2 = pl.program_id(0)
    kb = pl.program_id(1)
    rows = hi_ref.shape[1]
    points = own_points(points_ref, r2).astype(F32)
    inverse = 1.0 / points

    lane = iota((16, 128), 1).astype(F32)

    def chunk_body(i, carry):
        chunk = pl.multiple_of(i * 16, 16)

        def put(tile, value):
            lanes = slice(tile * 128, tile * 128 + 128)
            hi = value.astype(BF16)
            hi_ref[0, pl.ds(chunk, 16), lanes] = hi
            lo_ref[0, pl.ds(chunk, 16), lanes] = (value - hi.astype(F32)).astype(BF16)

        k = (kb * rows + chunk + iota((16, 128), 0)).astype(F32)
        c, s = unit_circle(2.0 * lane * k, points, inverse)
        c1, s1 = unit_circle(k, points, inverse)
        ct, st = unit_circle(256.0 * k, points, inverse)
        co = c * c1 - s * s1
        so = s * c1 + c * s1
        for t in range(HALF_M // 128):
            if t:
                c, s = c * ct - s * st, s * ct + c * st
                co, so = co * ct - so * st, so * ct + co * st
            put(t, c)
            put(5 + t, s)
            put(10 + t, co)
            put(15 + t, so)
        return carry

    lax.fori_loop(0, rows // 16, chunk_body, 0, unroll=True)


def tables(row_points):
    rows = KPTS // TABLE_STEPS
    table = pltpu.HBM((2, KPTS, 2 * M), BF16)
    table_spec = pl.BlockSpec((1, rows, 2 * M), lambda r, k: (r, k, 0))
    return pl.pallas_call(
        table_kernel,
        out_shape=[table, table],
        grid=(2, TABLE_STEPS),
        in_specs=[pl.BlockSpec(memory_space=pltpu.SMEM)],
        out_specs=[table_spec, table_spec],
        compiler_params=pltpu.CompilerParams(vmem_limit_bytes=48 * MIB),
        cost_estimate=pl.CostEstimate(flops=2 * KPTS * 2 * M * 12, bytes_accessed=2 * KPTS * 2 * M * 4, transcendentals=0),
        name="fourier_tables",
    )(pltpu.with_memory_space_constraint(row_points, pltpu.HBM))


def pick_tables(plev):
    wide = plev * 2 * PART
    out = np.zeros((2, 4, 2 * wide, 2 * wide), np.float32)
    plans = (
        ((0, 1), (0, 1), (0, 1), (0, 1)),
        ((1, -1), (1, 1), (1, -1), (1, 1)),
        ((0, 1), (0, 1), (1, -1), (1, -1)),
        ((1, -1), (1, 1), (0, -1), (0, 1)),
    )
    for r2 in range(2):
        for kind, plan in enumerate(plans):
            for image, (part, sgn) in enumerate(plan):
                for hl in range(2):
                    for p in range(plev):
                        for q in range(FS):
                            src = hl * wide + p * 2 * PART + r2 * PART + q * 2 + part
                            dst = hl * wide + image * plev * FS + p * FS + q
                            out[r2, kind, src, dst] = sgn
    return out.astype(jnp.bfloat16)


def mean_table(plev):
    wide = plev * FS * 4
    out = np.zeros((2 * 4 * plev, 2 * wide), np.float32)
    for quarter in range(4):
        for p in range(plev):
            for part in range(2):
                image_quarter = (quarter + part) % 4
                start = (image_quarter * 2 + part) * plev * FS + p * FS
                out[part * 4 * plev + quarter * plev + p, start : start + FS] = 0.5 / STEPS
    return out.astype(jnp.bfloat16)


def flip_table():
    return np.fliplr(np.eye(KBLK, dtype=np.float32)).astype(jnp.bfloat16)


def split(x):
    hi = x.astype(BF16)
    return hi, (x - hi.astype(F32)).astype(BF16)


def nt_dot(a, b):
    return lax.dot_general(a, b, (((1,), (1,)), ((), ())), preferred_element_type=F32)


def nn_dot(a, b):
    return jnp.dot(a, b, preferred_element_type=F32)


def synth_kernel(parts, points_ref, *refs):
    moved_ref, map_ref, pick_ref, mean_ref, flip_ref, hi_hbm, lo_hbm, out_ref = refs[:8]
    perm_ref, hi_ref, lo_ref, mixed, coef, flat, mirror, line, sems = refs[8:]
    table_copies = []
    for r2 in range(2):
        table_copies.append([])
        for i, (src, dst) in enumerate(((hi_hbm, hi_ref), (lo_hbm, lo_ref))):
            for c in range(TABLE_CUTS):
                rows = pl.ds(c * (KPTS // TABLE_CUTS), KPTS // TABLE_CUTS)
                table_copies[r2].append(pltpu.make_async_copy(src.at[r2, rows], dst.at[r2, rows], sems.at[r2, i, c]))
    for copy in table_copies[0]:
        copy.start()

    slot_waves = jnp.broadcast_to(map_ref[...], (16, M)).astype(jnp.int16)

    def perm_body(i, carry):
        row = pl.multiple_of(i * 16, 16)
        order = row + iota((16, M), 0)
        wanted = jnp.where(row < HALF_M, 2 * order, 2 * (order - HALF_M) + 1).astype(jnp.int16)
        perm_ref[pl.ds(row, 16), :] = jnp.where(slot_waves == wanted, 1.0, 0.0).astype(BF16)
        return carry

    lax.fori_loop(0, M // 16, perm_body, 0, unroll=4)
    waves, plev, _, _ = moved_ref.shape
    wide = plev * 2 * PART
    part_rows = M // SQ
    for base in range(0, plev * 2, 8):
        cur = []
        for g in range(base, base + 8):
            pieces = []
            for start, stop in parts:
                first = 2 * start + (g % 2) * (stop - start)
                pieces += [moved_ref[w, g // 2, first : first + stop - start, :] for w in range(waves)]
            cur.append(jnp.concatenate(pieces, axis=0))
        group = iota((part_rows, 128), 1) // PART
        for bit in (1, 2, 4):
            unset = (group & bit) == 0
            nxt = list(cur)
            for g in range(8):
                if g & bit == 0:
                    a, b = cur[g], cur[g + bit]
                    nxt[g] = jnp.where(unset, a, pltpu.roll(b, bit * PART, 1))
                    nxt[g + bit] = jnp.where(unset, pltpu.roll(a, 128 - bit * PART, 1), b)
            cur = nxt
        for sq in range(SQ):
            hi, lo = split(cur[sq])
            lane = base * PART
            mixed[sq * part_rows : (sq + 1) * part_rows, lane : lane + 128] = hi
            mixed[sq * part_rows : (sq + 1) * part_rows, wide + lane : wide + lane + 128] = lo

    lane_row = (iota((1, 2 * wide), 1) // PART) % 2
    limit0 = (own_points(points_ref, 0) - 1) // 2
    limit1 = (own_points(points_ref, 1) - 1) // 2
    limit = jnp.where(lane_row == 0, limit0, limit1)
    place = iota((HALF_M, 1), 0)
    turned = (iota((1, 2 * wide), 1) % wide) // (plev * FS) >= 2
    flip_sign = jnp.where(turned & (place % 2 == 1), -1.0, 1.0).astype(BF16)
    for odd in range(2):
        ordered = nn_dot(perm_ref[odd * HALF_M : (odd + 1) * HALF_M, :], mixed[...])
        wave = 2 * place + odd
        factor = jnp.where(wave <= limit, jnp.where(wave == 0, 1.0, 2.0), 0.0)
        ordered = (ordered * factor).astype(BF16)
        for row in range(2):
            for part in range(2):
                picked = nn_dot(ordered, pick_ref[row, odd * 2 + part]).astype(BF16)
                coef[row, odd, part * HALF_M : (part + 1) * HALF_M, :] = picked * flip_sign
    flat[...] = jnp.zeros_like(flat)
    mirror[...] = jnp.zeros_like(mirror)

    for r2 in range(2):
        for copy in table_copies[r2]:
            copy.wait()
        for copy in table_copies[1] if r2 == 0 else []:
            copy.start()

        def contraction(odd):
            lanes = slice(odd * M, (odd + 1) * M)
            both = nn_dot(hi_ref[r2, :, lanes], coef[r2, odd])
            rest = nn_dot(lo_ref[r2, :, lanes], coef[r2, odd, :, :wide])
            return both[:, :wide] + (both[:, wide:] + rest)

        even_sum = contraction(0)
        odd_sum = contraction(1)
        plus = even_sum + odd_sum
        minus = even_sum - odd_sum
        squares = jnp.concatenate([plus * plus, minus * minus], axis=1)
        sq_hi, sq_lo = split(squares)
        energy = nt_dot(mean_ref[...], sq_hi) + nt_dot(mean_ref[...], sq_lo)
        rows = 4 * plev
        flat[:, :KPTS] = energy
        en_hi, en_lo = split(flat[rows:, :KPAD])
        for t in range(KPAD // KBLK):
            lanes = slice(t * KBLK, (t + 1) * KBLK)
            back = KPAD - (t + 1) * KBLK
            mirror[:, back : back + KBLK] = nn_dot(en_hi[:, lanes], flip_ref[...]) + nn_dot(en_lo[:, lanes], flip_ref[...])

        quarter = own_points(points_ref, r2) // 4
        lane = iota((rows, BUF), 1)
        shift = (quarter + (BUF - (KPAD - 1))) % BUF
        flat[:rows, :] = jnp.where(lane <= quarter // 2, flat[:rows, :], pltpu.roll(mirror[...], shift, 1))
        line[...] = jnp.zeros_like(line)
        lane = iota((plev, BUF), 1)
        for b in range(4):
            start = quarter * b
            inner = start % 128
            base = pl.multiple_of(start - inner, 128)
            piece = pltpu.roll(flat[b * plev : (b + 1) * plev, :], inner, 1)
            old = line[:, pl.ds(base, BUF)]
            line[:, pl.ds(base, BUF)] = jnp.where((lane >= inner) & (lane < inner + quarter), piece, old)
        out_ref[:, pl.ds(r2, 1), :] = line[:, :ROWPAD].reshape(plev, 1, ROWPAD)


def synthesis(parts, moved, slot_map, table_hi, table_lo, row_points):
    plev = moved.shape[1]
    wide = plev * 2 * PART
    vmem = pl.BlockSpec(memory_space=pltpu.VMEM)
    return pl.pallas_call(
        functools.partial(synth_kernel, parts),
        out_shape=jax.ShapeDtypeStruct((plev, 2, ROWPAD), F32),
        in_specs=[pl.BlockSpec(memory_space=pltpu.SMEM)] + [vmem] * 5 + [pl.BlockSpec(memory_space=pltpu.HBM)] * 2,
        out_specs=vmem,
        scratch_shapes=[
            pltpu.VMEM((M, M), BF16),
            pltpu.VMEM((2, KPTS, 2 * M), BF16),
            pltpu.VMEM((2, KPTS, 2 * M), BF16),
            pltpu.VMEM((M, 2 * wide), BF16),
            pltpu.VMEM((2, 2, M, 2 * wide), BF16),
            pltpu.VMEM((8 * plev, BUF), F32),
            pltpu.VMEM((4 * plev, BUF), F32),
            pltpu.VMEM((plev, 3 * 1280 + BUF), F32),
            pltpu.SemaphoreType.DMA((2, 2, TABLE_CUTS)),
        ],
        compiler_params=pltpu.CompilerParams(vmem_limit_bytes=44 * MIB),
        cost_estimate=pl.CostEstimate(flops=2 * 2 * KPTS * 2 * M * 384, bytes_accessed=2 * KPTS * 2 * M * 4 + M * M * 2, transcendentals=0),
        name="synthesis",
    )(
        pltpu.with_memory_space_constraint(row_points, pltpu.HBM),
        pltpu.with_memory_space_constraint(moved, pltpu.VMEM), slot_map,
        pick_tables(plev), mean_table(plev), flip_table(),
        *[pltpu.with_memory_space_constraint(x, pltpu.HBM) for x in (table_hi, table_lo)],
    )


def join_kernel(*refs):
    parts = (len(refs) - 1) // 2
    at = 0
    for own_ref, other_ref in zip(refs[:parts], refs[parts:-1]):
        rows = own_ref.shape[1]
        refs[-1][:, at : at + rows, :] = own_ref[...] + other_ref[...]
        at += rows


def join(owns, others):
    rows = sum(x.shape[1] for x in owns)
    vmem = pl.BlockSpec(memory_space=pltpu.VMEM)
    return pl.pallas_call(
        join_kernel,
        out_shape=jax.ShapeDtypeStruct((owns[0].shape[0], rows, SQ * PART), F32),
        in_specs=[vmem] * (2 * len(owns)),
        out_specs=vmem,
        compiler_params=pltpu.CompilerParams(vmem_limit_bytes=32 * MIB),
        name="join",
    )(*[pltpu.with_memory_space_constraint(x, pltpu.VMEM) for x in owns + others])


def local(spectral, legendre, wave_map, row_points, brackets, lev_weight, climatology):
    slots = spectral.shape[0]
    half = legendre.shape[1]
    groups = slots // SQ
    wave_count = lax.axis_size("wave")
    lev_count = lax.axis_size("lev")
    rows_dev = 2 * half // (wave_count * lev_count)
    cuts = (0, groups)
    own_maps = wave_map.reshape(wave_count, SQ, groups)
    pairs = [(d, d - 1) for d in range(1, lev_count)]
    parts = list(zip(cuts[:-1], cuts[1:]))
    owns, others, maps = [], [], []
    order = wave_map
    for start, stop in parts:
        own, prev, between = legendre_sums(start, stop - start, spectral, legendre, order, brackets, lev_weight)
        order, prev = lax.optimization_barrier((wave_map, prev))
        owns.append(own)
        others.append(prev)
        maps.append(jnp.transpose(own_maps[:, :, start:stop], (1, 0, 2)).reshape(SQ, wave_count * (stop - start)))
    sent = lax.cond(
        between[0] > 0,
        lambda mine, theirs: join(mine, [lax.ppermute(x, "lev", pairs) for x in theirs]),
        lambda mine, theirs: join(mine, [lax.ppermute(x, "lev", pairs[::2]) for x in theirs]),
        owns,
        others,
    )
    moved = lax.all_to_all(sent, ("wave", "lev"), split_axis=0, concat_axis=0, tiled=True)
    moved = moved.reshape(wave_count, lev_count, rows_dev * groups, SQ * PART)
    slot_map = jnp.concatenate(maps, axis=1).reshape(1, M)
    table_points, _ = lax.optimization_barrier((row_points, sent))
    table_hi, table_lo = tables(table_points)
    energy = synthesis(parts, moved, slot_map, table_hi, table_lo, row_points)
    result = lax.all_to_all(energy, "lev", split_axis=0, concat_axis=0, tiled=True)
    result = result.reshape(1, rows_dev * lev_count, ROWPAD)
    points_all = jnp.concatenate([row_points, row_points])
    band_rows = rows_dev * lev_count
    out_points = lax.dynamic_slice_in_dim(points_all, lax.axis_index("wave") * band_rows, band_rows, 0)
    places = jnp.arange(ROWPAD, dtype=jnp.int32)
    inside = places[None, None, :] < out_points[None, :, None]
    return jnp.where(inside, result - climatology, 0.0)


def solution(mesh):
    placed = (
        P("wave", "lev", None),
        P("wave", None, None),
        P(),
        P(),
        P(),
        P(),
        P("lev", "wave", None),
    )
    return jax.shard_map(
        local, mesh=mesh, in_specs=placed, out_specs=P("lev", "wave", None), check_vma=False
    )
```

profile of v0, /device:TPU:0, one launch (start us, length us, event | category | flops | bytes accessed | tf_op | source)
XLA Modules:
  0.0 73.2 jit_solution(1612071127491232239)
XLA Ops:
  0.0 0.0 copy-start.4
  0.0 0.0 copy-start
  0.0 0.0 copy-start.1
  0.0 0.0 copy-start.2
  0.0 14.4 %legendre_sums.1 = (f32[32,40,128]{2,1,0:T(8,128)S(1)}, f32[32,40,128]{2,1,0:T(8,128)S(1)}, s32[1]{0:T(128)}) custom-call(s32[1280]{0:T(1024)} %wave_map.1, s32[4]{0:T(128)} %brackets.1, f32[4]{0:T(128)} %weight_ref.1, bf16[8,20,64,1280]{3,2,1,0:T(8,128)(2,1)} %bitcast.6, bf16[8,20,32,1280]{3,2,1,0:T(8,128)(2,1)} %bitcast.7), custom_call_target="tpu_custom_call" | custom-call | flops 1258291200 | bytes 32768000 | tf_op jit(solution)/shard_map/legendre_sums/pallas_call | solution.py:151
  14.4 0.0 copy-start.5
  14.4 0.0 copy-start.3
  15.1 4.9 %conditional.1 = (f32[32,40,128]{2,1,0:T(8,128)}) conditional(s32[]{:T(128)} %bitcast.2, (f32[32,40,128]{2,1,0:T(8,128)S(1)}, f32[32,40,128]{2,1,0:T(8,128)S(1)}) %tuple.14, (f32[32,40,128]{2,1,0:T(8,128)S(1)}, f32[32,40,128]{2,1,0:T(8,128)S(1)}) %tuple.14), branch_computations={%region_0.0_spmd, %region_1.0_spmd} | conditional | bytes 2621488 | solution.py:480
  15.1 1.3 %collective-permute-start.1 = (f32[32,40,128]{2,1,0:T(8,128)S(1)}, f32[32,40,128]{2,1,0:T(8,128)S(1)}, u32[]{:S(2)}, u32[]{:S(2)}) collective-permute-start(f32[32,40,128]{2,1,0:T(8,128)S(1)} %get-tuple-element.19), channel_id=1, source_target_pairs={{1,0},{2,1},{3,2},{5,4},{6,5},{7,6},{9,8},{10,9},{11,10},{13,12},{... | collective-permute-start | bytes 1966088 | tf_op jit(solution)/shard_map/cond/branch_1_fun/ppermute | solution.py:482
  16.4 2.7 %collective-permute-done.1.refs_1_ = f32[32,40,128]{2,1,0:T(8,128)S(1)} collective-permute-done((f32[32,40,128]{2,1,0:T(8,128)S(1)}, f32[32,40,128]{2,1,0:T(8,128)S(1)}, u32[]{:S(2)}, u32[]{:S(2)}) %collective-permute-start.1) | collective-permute-done | bytes 655392 | tf_op jit(solution)/shard_map/cond/branch_1_fun/ppermute | solution.py:482
  19.1 0.9 %join.3 = f32[32,40,128]{2,1,0:T(8,128)} custom-call(f32[32,40,128]{2,1,0:T(8,128)S(1)} %get-tuple-element.18.refs_0_, f32[32,40,128]{2,1,0:T(8,128)S(1)} %collective-permute-done.1.refs_1_), custom_call_target="tpu_custom_call" | custom-call | tf_op jit(solution)/shard_map/cond/branch_1_fun/join/pallas_call | solution.py:451
  20.0 13.7 %all-to-all-start = ((f32[32,40,128]{2,1,0:T(8,128)}), f32[32,40,128]{2,1,0:T(8,128)S(1)}, u32[]{:S(2)}, u32[]{:S(2)}) async-start(f32[32,40,128]{2,1,0:T(8,128)} %get-tuple-element.34), calls=%async_computation | async-start | bytes 1310720 | tf_op jit(solution)/shard_map/all_to_all | solution.py:487
  33.8 0.0 copy-done.4
  33.8 0.1 reshape.54
  33.9 0.1 reshape_reshape.3.refs_1_
  34.0 11.3 %fourier_tables.1 = (bf16[2,672,2560]{2,1,0:T(8,128)(2,1)}, bf16[2,672,2560]{2,1,0:T(8,128)(2,1)}) custom-call(s32[32]{0:T(128)} %points_ref.2), custom_call_target="tpu_custom_call" | custom-call | flops 41287680 | bytes 13762560 | tf_op jit(solution)/shard_map/fourier_tables/pallas_call | solution.py:234
  45.4 6.3 %all-to-all-done = f32[32,40,128]{2,1,0:T(8,128)S(1)} async-done(((f32[32,40,128]{2,1,0:T(8,128)}), f32[32,40,128]{2,1,0:T(8,128)S(1)}, u32[]{:S(2)}, u32[]{:S(2)}) %all-to-all-start) | async-done | bytes 655392 | tf_op jit(solution)/shard_map/all_to_all | solution.py:487
  51.7 0.0 copy-done
  51.7 0.0 copy-done.1
  51.7 0.0 copy-done.2
  51.7 12.3 %synthesis.1 = f32[4,2,5248]{2,1,0:T(2,128)} custom-call(s32[32]{0:T(128)} %points_ref.2, f32[8,4,40,128]{3,2,1,0:T(8,128)S(1)} %bitcast.5, s32[1,1280]{1,0:T(1,128)S(1)} %reshape_reshape.3.refs_1_, bf16[2,4,256,256]{3,2,1,0:T(8,128)(2,1)S(1)} %copy-done, bf16[32,256]{1,0:T(8,128)(2,1)S(1)} %copy-done.2, bf16[256,256]{1,0:T(8,128)(2,1)S(1)} %copy-done.1, ...), custom_call_target="tpu_custom_call" | custom-call | flops 2642411520 | bytes 17039360 | tf_op jit(solution)/shard_map/synthesis/pallas_call | solution.py:412
  64.0 3.4 %all-to-all-start.1 = ((f32[4,2,5248]{2,1,0:T(2,128)}), f32[4,2,5248]{2,1,0:T(2,128)S(1)}, u32[]{:S(2)}, u32[]{:S(2)}) async-start(f32[4,2,5248]{2,1,0:T(2,128)} %synthesis.1), calls=%async_computation.1 | async-start | bytes 335872 | tf_op jit(solution)/shard_map/all_to_all | solution.py:493
  67.4 0.0 copy-done.5
  67.4 0.1 pad_add_fusion
  67.4 0.1 dynamic_slice.3
  67.5 4.8 %all-to-all-done.1 = f32[4,2,5248]{2,1,0:T(2,128)S(1)} async-done(((f32[4,2,5248]{2,1,0:T(2,128)}), f32[4,2,5248]{2,1,0:T(2,128)S(1)}, u32[]{:S(2)}, u32[]{:S(2)}) %all-to-all-start.1) | async-done | bytes 167968 | tf_op jit(solution)/shard_map/all_to_all | solution.py:493
  72.4 0.1 reshape.55
  72.5 0.0 copy-done.3
  72.5 0.8 %subtract_select_fusion = f32[1,8,5248]{2,1,0:T(8,128)} fusion(f32[1,8,5248]{2,1,0:T(8,128)S(1)} %reshape.55, f32[1,8,5248]{2,1,0:T(8,128)S(1)} %copy-done.3, s32[8]{0:T(128)S(1)} %dynamic_slice.3), kind=kLoop, calls=%fused_computation | loop fusion | flops 125952 | bytes 503840 | tf_op jit(solution)/shard_map/jit(_where)/select_n | solution.py:500
  (1 shorter events, 0.0 us)
Async XLA Ops:
  0.0 33.8 %copy-start.4 = (s32[1280]{0:T(1024)S(1)}, s32[1280]{0:T(1024)}, u32[]{:S(2)}) copy-start(s32[1280]{0:T(1024)} %wave_map.1) | copy-start | bytes 15364
  0.0 51.7 %copy-start = (bf16[2,4,256,256]{3,2,1,0:T(8,128)(2,1)S(1)}, bf16[2,4,256,256]{3,2,1,0:T(8,128)(2,1)}, u32[]{:S(2)}) copy-start(bf16[2,4,256,256]{3,2,1,0:T(8,128)(2,1)} %constant.22.clone.refs_2_) | copy-start | bytes 3145732
  0.0 51.7 %copy-start.1 = (bf16[256,256]{1,0:T(8,128)(2,1)S(1)}, bf16[256,256]{1,0:T(8,128)(2,1)}, u32[]{:S(2)}) copy-start(bf16[256,256]{1,0:T(8,128)(2,1)} %constant.24.clone.refs_4_) | copy-start | bytes 393220
  0.0 51.7 %copy-start.2 = (bf16[32,256]{1,0:T(8,128)(2,1)S(1)}, bf16[32,256]{1,0:T(8,128)(2,1)}, u32[]{:S(2)}) copy-start(bf16[32,256]{1,0:T(8,128)(2,1)} %constant.23.clone.refs_3_) | copy-start | bytes 49156
  14.4 53.0 %copy-start.5 = (s32[32]{0:T(128)S(1)}, s32[32]{0:T(128)}, u32[]{:S(2)}) copy-start(s32[32]{0:T(128)} %points_ref.2) | copy-start | bytes 388
  14.4 58.1 %copy-start.3 = (f32[1,8,5248]{2,1,0:T(8,128)S(1)}, f32[1,8,5248]{2,1,0:T(8,128)}, u32[]{:S(2)}) copy-start(f32[1,8,5248]{2,1,0:T(8,128)} %param.18) | copy-start | bytes 503812
  15.1 4.0 %collective-permute-start.1 = (f32[32,40,128]{2,1,0:T(8,128)S(1)}, f32[32,40,128]{2,1,0:T(8,128)S(1)}, u32[]{:S(2)}, u32[]{:S(2)}) collective-permute-start(f32[32,40,128]{2,1,0:T(8,128)S(1)} %get-tuple-element.19), channel_id=1, source_target_pairs={{1,0},{2,1},{3,2},{5,4},{6,5},{7,6},{9,8},{10,9},{11,10},{13,12},{... | collective-permute-start | bytes 1966088 | tf_op jit(solution)/shard_map/cond/branch_1_fun/ppermute | solution.py:482
  20.0 31.7 %all-to-all-start = ((f32[32,40,128]{2,1,0:T(8,128)}), f32[32,40,128]{2,1,0:T(8,128)S(1)}, u32[]{:S(2)}, u32[]{:S(2)}) async-start(f32[32,40,128]{2,1,0:T(8,128)} %get-tuple-element.34), calls=%async_computation | async-start | bytes 1310720 | tf_op jit(solution)/shard_map/all_to_all | solution.py:487
  64.0 8.4 %all-to-all-start.1 = ((f32[4,2,5248]{2,1,0:T(2,128)}), f32[4,2,5248]{2,1,0:T(2,128)S(1)}, u32[]{:S(2)}, u32[]{:S(2)}) async-start(f32[4,2,5248]{2,1,0:T(2,128)} %synthesis.1), calls=%async_computation.1 | async-start | bytes 335872 | tf_op jit(solution)/shard_map/all_to_all | solution.py:493
where the time goes:
time: 73.6 us; the launch traced here: 73.2 us
  Pallas kernels  38.9 us (53%)
  starting transfers between devices  18.4 us (25%)
  waiting for transfers between devices  13.9 us (19%)
  other arithmetic  0.83 us (1%)
  between operations  0.8 us (1%)
    pallas_call x1, Pallas kernels, legendre_sums(): pl.pallas_call(functools.partial(legendre_kernel, first_group, count), ou...  14.4 us
    all_to_all x1, starting transfers between devices, local(): lax.all_to_all(sent, ('wave', 'lev'), split_axis=0, concat_axis=0, tiled=...  13.7 us
    pallas_call x1, Pallas kernels, synthesis(): pl.pallas_call(functools.partial(synth_kernel, parts), out_shape=jax.Shap...  12.3 us
    pallas_call x1, Pallas kernels, tables(): pl.pallas_call(table_kernel, out_shape=[table, table], grid=(2, TABLE_STE...  11.3 us
    all_to_all x1, waiting for transfers between devices, local(): lax.all_to_all(sent, ('wave', 'lev'), split_axis=0, concat_axis=0, tiled=...  6.34 us
    all_to_all x1, waiting for transfers between devices, local(): lax.all_to_all(energy, 'lev', split_axis=0, concat_axis=0, tiled=True)  4.82 us
    all_to_all x1, starting transfers between devices, local(): lax.all_to_all(energy, 'lev', split_axis=0, concat_axis=0, tiled=True)  3.36 us
    ppermute x1, waiting for transfers between devices, local(): lax.ppermute(x, 'lev', pairs)  2.69 us
  transfers between devices with their start and end apart: 3, of which 3 were waited for; matrix products, arithmetic and copies ran while one was open for 0% of the time, Pallas kernels for 15%

commit v1 on v0

--- a/solution.py
+++ b/solution.py
@@ -19,6 +19,8 @@
 FS = FIELDS * STEPS
 PART = 2 * FS
 SQ = 8
+STEP = 16
+CHUNK = 256
 DEPTH = 3
 HALF_M = M // 2
 KPTS = 672
@@ -36,54 +38,75 @@
     return lax.broadcasted_iota(jnp.int32, shape, dim)
 
 
+def waves_of(map_ref, wave, slots):
+    start = wave * slots
+    row = start // 128
+    last = map_ref.shape[0] - 1
+    pair = jnp.concatenate([map_ref[pl.ds(row, 1), :], map_ref[pl.ds(jnp.minimum(row + 1, last), 1), :]], axis=1)
+    pair = jnp.broadcast_to(pair, (8, 256)).astype(F32)
+    turned = pltpu.roll(pair, (256 - start % 128) % 256, 1)
+    return jnp.where(iota((8, 256), 1) < slots, turned, 4096.0)[:1]
+
+
+def ranks_of(waves):
+    across = jnp.broadcast_to(waves, (256, 256))
+    down = across.T
+    rank = jnp.sum(jnp.where(across < down, 1.0, 0.0), axis=1, keepdims=True)
+    return rank, down
+
+
 def legendre_kernel(
-    first_group, count, wave_map, brackets, weight_ref, spec_hbm, leg_hbm, own_ref, prev_ref, between_ref,
-    low_buf, up_buf, first_buf, leg_buf, own_rows, prev_rows, sems,
+    brackets, weight_ref, map_ref, spec_hbm, leg_hbm, own_ref, prev_ref, between_ref,
+    pair_buf, first_buf, leg_buf, own_rows, prev_rows, order_vmem, order, order_sem, sems,
 ):
-    groups = spec_hbm.shape[1]
-    slots = SQ * groups
-    step_slots = low_buf.shape[2]
-    steps = count // step_slots
-    half = leg_hbm.shape[2]
+    slots, half, _ = leg_hbm.shape
+    groups = slots // SQ
+    steps = slots // STEP
     wave = lax.axis_index("wave")
     lev = lax.axis_index("lev")
     lower = brackets[lev] - lev * LEV_DEV
     has_upper = lower < LEV_DEV - 1
     w = weight_ref[lev]
-    upper_w = jnp.where(has_upper, 1.0 - w, 0.0)
+    low_w = jnp.where(has_upper, w, 0.0)
+    upper_w = jnp.where(has_upper, 1.0 - w, w)
+    pair_row = jnp.minimum(lower, LEV_DEV - 2) * PART
     before = jnp.maximum(lev - 1, 0)
     crosses = (lev > 0) & (brackets[before] == lev * LEV_DEV - 1)
     first_w = jnp.where(crosses, 1.0 - weight_ref[before], 0.0)
     degree = iota((16, NT), 1).astype(jnp.int16)
     sign = (1 - 2 * (iota((16, NT), 1) % 2)).astype(F32).astype(BF16)
-    lane_group = iota((1, 2 * SQ * PART), 1) % 64 // PART
+    lane_group = iota((1, 192), 1) % 64 // PART
     left = iota((1, SQ * PART), 1) < 64
     south = iota((2 * half, 1), 0) >= half
 
-    def columns_copy(step, level, buf, kind):
-        slot = step % DEPTH
-        rows = pl.ds(pl.multiple_of(level * PART, PART), PART)
-        src = spec_hbm.at[:, pl.ds(first_group + step * step_slots, step_slots), rows, :]
-        return pltpu.make_async_copy(src, buf.at[slot], sems.at[slot, kind])
-
-    def values_copy(step):
-        slot = step % DEPTH
-        src = leg_hbm.at[:, pl.ds(first_group + step * step_slots, step_slots)]
-        return pltpu.make_async_copy(src, leg_buf.at[slot], sems.at[slot, 3])
-
-    upper = jnp.minimum(lower + 1, LEV_DEV - 1)
-
-    def copies(step):
+    rank, down = ranks_of(waves_of(map_ref, wave, slots))
+    hit = rank == iota((256, 256), 1).astype(F32)
+    slot_at = jnp.sum(jnp.where(hit, iota((256, 256), 0).astype(F32), 0.0), axis=0, keepdims=True)
+    wave_at = jnp.sum(jnp.where(hit, down, 0.0), axis=0, keepdims=True)
+    order_vmem[0:1, :] = slot_at.astype(jnp.int32)
+    order_vmem[1:2, :] = wave_at.astype(jnp.int32)
+    to_smem = pltpu.make_async_copy(order_vmem, order, order_sem)
+    to_smem.start()
+    to_smem.wait()
+
+    def buffers(slot, c):
+        lanes = pl.ds(c * CHUNK, NT - c * CHUNK)
         return [
-            values_copy(step),
-            columns_copy(step, lower, low_buf, 0),
-            columns_copy(step, upper, up_buf, 1),
-            columns_copy(step, 0, first_buf, 2),
+            (leg_hbm.at[:, :, lanes], leg_buf.at[slot, :, :, lanes], sems.at[slot, 0]),
+            (spec_hbm.at[:, pl.ds(pl.multiple_of(pair_row, PART), 2 * PART), lanes], pair_buf.at[slot, :, :, lanes], sems.at[slot, 1]),
+            (spec_hbm.at[:, pl.ds(0, PART), lanes], first_buf.at[slot, :, :, lanes], sems.at[slot, 2]),
         ]
 
     def fetch(step):
-        for copy in copies(step):
-            copy.start()
+        chunk = order[1, step * STEP] // CHUNK
+        for c in range(NT // CHUNK):
+
+            @pl.when(chunk == c)
+            def _():
+                for i in range(STEP):
+                    at = order[0, step * STEP + i]
+                    for src, dst, sem in buffers(step % DEPTH, c):
+                        pltpu.make_async_copy(src.at[at], dst.at[i], sem).start()
 
     for step in range(DEPTH - 1):
         fetch(step)
@@ -92,79 +115,84 @@
         between = between | (brackets[p] == (p + 1) * LEV_DEV - 1).astype(jnp.int32)
     between_ref[0] = between
 
+    def multiply(step, c):
+        slot = step % DEPTH
+        lanes = slice(c * CHUNK, NT)
+        for src, dst, sem in buffers(slot, c):
+            pltpu.make_async_copy(src.at[pl.ds(0, STEP)], dst, sem).wait()
+        for b in range(STEP // SQ):
+            owns, firsts = [], []
+            for quad in range(2):
+                values, factors, columns = [], [], [[], [], []]
+                for i in range(b * SQ + 4 * quad, b * SQ + 4 * quad + 4):
+                    m = order[1, step * STEP + i]
+                    kept = degree[:, lanes] >= m.astype(jnp.int16)
+                    plain = [jnp.where(kept, leg_buf[slot, i, r : r + 16, lanes], 0) for r in range(0, half, 16)]
+                    values += plain + [x * sign[:, lanes] for x in plain]
+                    factors.append(jnp.where(south, (1 - 2 * (m % 2)).astype(F32), 1.0))
+                    columns[quad].append(pair_buf[slot, i, :PART, lanes])
+                    columns[1 - quad].append(pair_buf[slot, i, PART:, lanes])
+                    columns[2].append(first_buf[slot, i, :, lanes])
+                sums = nt_dot(jnp.concatenate(values, axis=0), jnp.concatenate(columns[0] + columns[1] + columns[2], axis=0))
+                kept_sums = sums[: 2 * half] * factors[0]
+                for a in range(1, 4):
+                    block = sums[2 * half * a : 2 * half * (a + 1)] * factors[a]
+                    kept_sums = jnp.where(lane_group == a, block, kept_sums)
+                both = kept_sums[:, :128]
+                owns.append(both * low_w + pltpu.roll(both, 64, 1) * upper_w)
+                firsts.append(jnp.concatenate([kept_sums[:, 128:]] * 2, axis=1))
+            at = pl.multiple_of((step * (STEP // SQ) + b) * 2 * half, 2 * half)
+            own_rows[pl.ds(at, 2 * half), :] = jnp.where(left, owns[0], owns[1])
+            prev_rows[pl.ds(at, 2 * half), :] = jnp.where(left, firsts[0], firsts[1]) * first_w
+
     def step_body(step, carry):
-        slot = step % DEPTH
-        for copy in copies(step):
-            copy.wait()
-
         @pl.when(step + DEPTH - 1 < steps)
         def _():
             fetch(step + DEPTH - 1)
 
-        for b in range(step_slots):
-            owns, firsts = [], []
-            for quad in range(2):
-                values, factors = [], []
-                for sq in range(4 * quad, 4 * quad + 4):
-                    m = wave_map[wave * slots + sq * groups + first_group + step * step_slots + b]
-                    kept = degree >= m.astype(jnp.int16)
-                    plain = [jnp.where(kept, leg_buf[slot, sq, b, i : i + 16, :], 0) for i in range(0, half, 16)]
-                    values += plain + [x * sign for x in plain]
-                    factors.append(jnp.where(south, (1 - 2 * (m % 2)).astype(F32), 1.0))
-                bufs = (low_buf, up_buf, first_buf) if quad == 0 else (up_buf, low_buf, first_buf)
-                columns = [buf[slot, sq, b] for buf in bufs for sq in range(4 * quad, 4 * quad + 4)]
-                sums = nt_dot(jnp.concatenate(values, axis=0), jnp.concatenate(columns, axis=0))
-                kept_sums = sums[: 2 * half] * factors[0]
-                for a in range(1, 4):
-                    block = sums[2 * half * a : 2 * half * (a + 1)] * factors[a]
-                    kept_sums = jnp.where(lane_group[:, :192] == a, block, kept_sums)
-                both = kept_sums[:, :128]
-                other = pltpu.roll(both, 64, 1)
-                owns.append(both * w + other * upper_w)
-                firsts.append(jnp.concatenate([kept_sums[:, 128:]] * 2, axis=1))
-            at = pl.multiple_of((step * step_slots + b) * 2 * half, 2 * half)
-            own_rows[pl.ds(at, 2 * half), :] = jnp.where(left, owns[0], owns[1])
-            prev_rows[pl.ds(at, 2 * half), :] = jnp.where(left, firsts[0], firsts[1]) * first_w
+        chunk = order[1, step * STEP] // CHUNK
+        for c in range(NT // CHUNK):
+            pl.when(chunk == c)(functools.partial(multiply, step, c))
         return carry
 
     lax.fori_loop(0, steps, step_body, 0)
     rows = 2 * half
     for rows_ref, ref in ((own_rows, own_ref), (prev_rows, prev_ref)):
-        rows_dev = ref.shape[1] // count
+        rows_dev = ref.shape[1] // groups
         for r in range(rows):
-            at = (r % rows_dev) * count
-            ref[r // rows_dev, at : at + count, :] = rows_ref[pl.ds(r, count, stride=rows), :]
-
-
-def legendre_sums(first_group, count, spectral, legendre, wave_map, brackets, lev_weight):
-    slots, cols, _ = spectral.shape
+            at = (r % rows_dev) * groups
+            ref[r // rows_dev, at : at + groups, :] = rows_ref[pl.ds(r, groups, stride=rows), :]
+
+
+def legendre_sums(spectral, legendre, map_rows, brackets, lev_weight):
+    slots = spectral.shape[0]
     half = legendre.shape[1]
     groups = slots // SQ
-    step_slots = 4 if count % 4 == 0 else 2
-    spec = spectral.reshape(SQ, groups, cols, NT)
-    leg = legendre.reshape(SQ, groups, half, NT)
     devices = lax.axis_size("wave") * lax.axis_size("lev")
-    out = pltpu.VMEM((devices, 2 * half // devices * count, SQ * PART), F32)
+    out = pltpu.VMEM((devices, 2 * half // devices * groups, SQ * PART), F32)
     smem = pl.BlockSpec(memory_space=pltpu.SMEM)
     vmem = pl.BlockSpec(memory_space=pltpu.VMEM)
-    anywhere = pl.BlockSpec(memory_space=pltpu.HBM)
+    hbm = pl.BlockSpec(memory_space=pltpu.HBM)
     return pl.pallas_call(
-        functools.partial(legendre_kernel, first_group, count),
+        legendre_kernel,
         out_shape=[out, out, jax.ShapeDtypeStruct((1,), jnp.int32)],
-        in_specs=[smem, smem, smem, anywhere, anywhere],
+        in_specs=[smem, smem, vmem, hbm, hbm],
         out_specs=[vmem, vmem, smem],
-        scratch_shapes=[pltpu.VMEM((DEPTH, SQ, step_slots, PART, NT), BF16)] * 3
-        + [pltpu.VMEM((DEPTH, SQ, step_slots, half, NT), BF16)]
-        + [pltpu.VMEM((count * 2 * half, SQ * PART), F32)] * 2
-        + [pltpu.SemaphoreType.DMA((DEPTH, 4))],
+        scratch_shapes=[
+            pltpu.VMEM((DEPTH, STEP, 2 * PART, NT), BF16),
+            pltpu.VMEM((DEPTH, STEP, PART, NT), BF16),
+            pltpu.VMEM((DEPTH, STEP, half, NT), BF16),
+            pltpu.VMEM((groups * 2 * half, SQ * PART), F32),
+            pltpu.VMEM((groups * 2 * half, SQ * PART), F32),
+            pltpu.VMEM((2, 256), jnp.int32),
+            pltpu.SMEM((2, 256), jnp.int32),
+            pltpu.SemaphoreType.DMA,
+            pltpu.SemaphoreType.DMA((DEPTH, 3)),
+        ],
         compiler_params=pltpu.CompilerParams(vmem_limit_bytes=48 * MIB),
-        cost_estimate=pl.CostEstimate(
-            flops=2 * SQ * count * 2 * half * 48 * NT, bytes_accessed=SQ * count * NT * 2 * (48 + half), transcendentals=0
-        ),
+        cost_estimate=pl.CostEstimate(flops=2 * slots * 2 * half * 48 * NT, bytes_accessed=slots * NT * 2 * (48 + half), transcendentals=0),
         name="legendre_sums",
-    )(
-        *[pltpu.with_memory_space_constraint(x, pltpu.HBM) for x in (wave_map, brackets, lev_weight, spec, leg)]
-    )
+    )(*[pltpu.with_memory_space_constraint(x, pltpu.HBM) for x in (brackets, lev_weight, map_rows, spectral, legendre)])
 
 
 def unit_circle(product, points, inverse):
@@ -190,12 +218,23 @@
     return points_ref[row % points_ref.shape[0]]
 
 
-def table_kernel(points_ref, hi_ref, lo_ref):
+def table_kernel(points_ref, map_ref, hi_ref, lo_ref, sorted_ref):
     r2 = pl.program_id(0)
     kb = pl.program_id(1)
     rows = hi_ref.shape[1]
     points = own_points(points_ref, r2).astype(F32)
     inverse = 1.0 / points
+
+    @pl.when((r2 == 0) & (kb == 0))
+    def _():
+        waves, slots = sorted_ref.shape
+        for wave in range(waves):
+            rank, down = ranks_of(waves_of(map_ref, wave, slots))
+            whole = jnp.floor((rank + 0.5) * (1.0 / SQ))
+            place = (rank - whole * SQ) * (slots // SQ) + whole
+            hit = (place == iota((256, 256), 1).astype(F32)) & (rank < slots)
+            row = jnp.sum(jnp.where(hit, down, 0.0), axis=0, keepdims=True)
+            sorted_ref[wave : wave + 1, :] = row[:, :slots].astype(jnp.int32)
 
     lane = iota((16, 128), 1).astype(F32)
 
@@ -227,20 +266,21 @@
     lax.fori_loop(0, rows // 16, chunk_body, 0, unroll=True)
 
 
-def tables(row_points):
+def tables(row_points, map_rows):
+    waves = lax.axis_size("wave")
     rows = KPTS // TABLE_STEPS
     table = pltpu.HBM((2, KPTS, 2 * M), BF16)
     table_spec = pl.BlockSpec((1, rows, 2 * M), lambda r, k: (r, k, 0))
     return pl.pallas_call(
         table_kernel,
-        out_shape=[table, table],
+        out_shape=[table, table, jax.ShapeDtypeStruct((waves, M // waves), jnp.int32)],
         grid=(2, TABLE_STEPS),
-        in_specs=[pl.BlockSpec(memory_space=pltpu.SMEM)],
-        out_specs=[table_spec, table_spec],
+        in_specs=[pl.BlockSpec(memory_space=pltpu.SMEM), pl.BlockSpec(memory_space=pltpu.VMEM)],
+        out_specs=[table_spec, table_spec, pl.BlockSpec(memory_space=pltpu.VMEM)],
         compiler_params=pltpu.CompilerParams(vmem_limit_bytes=48 * MIB),
         cost_estimate=pl.CostEstimate(flops=2 * KPTS * 2 * M * 12, bytes_accessed=2 * KPTS * 2 * M * 4, transcendentals=0),
         name="fourier_tables",
-    )(pltpu.with_memory_space_constraint(row_points, pltpu.HBM))
+    )(*[pltpu.with_memory_space_constraint(x, pltpu.HBM) for x in (row_points, map_rows)])
 
 
 def pick_tables(plev):
@@ -293,7 +333,7 @@
     return jnp.dot(a, b, preferred_element_type=F32)
 
 
-def synth_kernel(parts, points_ref, *refs):
+def synth_kernel(points_ref, *refs):
     moved_ref, map_ref, pick_ref, mean_ref, flip_ref, hi_hbm, lo_hbm, out_ref = refs[:8]
     perm_ref, hi_ref, lo_ref, mixed, coef, flat, mirror, line, sems = refs[8:]
     table_copies = []
@@ -322,10 +362,8 @@
     for base in range(0, plev * 2, 8):
         cur = []
         for g in range(base, base + 8):
-            pieces = []
-            for start, stop in parts:
-                first = 2 * start + (g % 2) * (stop - start)
-                pieces += [moved_ref[w, g // 2, first : first + stop - start, :] for w in range(waves)]
+            sub = moved_ref.shape[2] // 2
+            pieces = [moved_ref[w, g // 2, (g % 2) * sub : (g % 2 + 1) * sub, :] for w in range(waves)]
             cur.append(jnp.concatenate(pieces, axis=0))
         group = iota((part_rows, 128), 1) // PART
         for bit in (1, 2, 4):
@@ -362,6 +400,7 @@
     flat[...] = jnp.zeros_like(flat)
     mirror[...] = jnp.zeros_like(mirror)
 
+    row_sums = []
     for r2 in range(2):
         for copy in table_copies[r2]:
             copy.wait()
@@ -374,8 +413,10 @@
             rest = nn_dot(lo_ref[r2, :, lanes], coef[r2, odd, :, :wide])
             return both[:, :wide] + (both[:, wide:] + rest)
 
-        even_sum = contraction(0)
-        odd_sum = contraction(1)
+        row_sums.append((contraction(0), contraction(1)))
+
+    for r2 in range(2):
+        even_sum, odd_sum = row_sums[r2]
         plus = even_sum + odd_sum
         minus = even_sum - odd_sum
         squares = jnp.concatenate([plus * plus, minus * minus], axis=1)
@@ -405,12 +446,12 @@
         out_ref[:, pl.ds(r2, 1), :] = line[:, :ROWPAD].reshape(plev, 1, ROWPAD)
 
 
-def synthesis(parts, moved, slot_map, table_hi, table_lo, row_points):
+def synthesis(moved, slot_map, table_hi, table_lo, row_points):
     plev = moved.shape[1]
     wide = plev * 2 * PART
     vmem = pl.BlockSpec(memory_space=pltpu.VMEM)
     return pl.pallas_call(
-        functools.partial(synth_kernel, parts),
+        synth_kernel,
         out_shape=jax.ShapeDtypeStruct((plev, 2, ROWPAD), F32),
         in_specs=[pl.BlockSpec(memory_space=pltpu.SMEM)] + [vmem] * 5 + [pl.BlockSpec(memory_space=pltpu.HBM)] * 2,
         out_specs=vmem,
@@ -465,31 +506,22 @@
     wave_count = lax.axis_size("wave")
     lev_count = lax.axis_size("lev")
     rows_dev = 2 * half // (wave_count * lev_count)
-    cuts = (0, groups)
-    own_maps = wave_map.reshape(wave_count, SQ, groups)
     pairs = [(d, d - 1) for d in range(1, lev_count)]
-    parts = list(zip(cuts[:-1], cuts[1:]))
-    owns, others, maps = [], [], []
-    order = wave_map
-    for start, stop in parts:
-        own, prev, between = legendre_sums(start, stop - start, spectral, legendre, order, brackets, lev_weight)
-        order, prev = lax.optimization_barrier((wave_map, prev))
-        owns.append(own)
-        others.append(prev)
-        maps.append(jnp.transpose(own_maps[:, :, start:stop], (1, 0, 2)).reshape(SQ, wave_count * (stop - start)))
+    map_rows = wave_map.reshape(M // 128, 128)
+    own, prev, between = legendre_sums(spectral, legendre, map_rows, brackets, lev_weight)
     sent = lax.cond(
         between[0] > 0,
-        lambda mine, theirs: join(mine, [lax.ppermute(x, "lev", pairs) for x in theirs]),
-        lambda mine, theirs: join(mine, [lax.ppermute(x, "lev", pairs[::2]) for x in theirs]),
-        owns,
-        others,
+        lambda mine, theirs: join([mine], [lax.ppermute(theirs, "lev", pairs)]),
+        lambda mine, theirs: join([mine], [lax.ppermute(theirs, "lev", pairs[::2])]),
+        own,
+        prev,
     )
     moved = lax.all_to_all(sent, ("wave", "lev"), split_axis=0, concat_axis=0, tiled=True)
     moved = moved.reshape(wave_count, lev_count, rows_dev * groups, SQ * PART)
-    slot_map = jnp.concatenate(maps, axis=1).reshape(1, M)
     table_points, _ = lax.optimization_barrier((row_points, sent))
-    table_hi, table_lo = tables(table_points)
-    energy = synthesis(parts, moved, slot_map, table_hi, table_lo, row_points)
+    table_hi, table_lo, sorted_map = tables(table_points, map_rows)
+    slot_map = jnp.transpose(sorted_map.reshape(wave_count, SQ, groups), (1, 0, 2)).reshape(1, M)
+    energy = synthesis(moved, slot_map, table_hi, table_lo, row_points)
     result = lax.all_to_all(energy, "lev", split_axis=0, concat_axis=0, tiled=True)
     result = result.reshape(1, rows_dev * lev_count, ROWPAD)
     points_all = jnp.concatenate([row_points, row_points])

time: 73.6 us -> 72.9 us (level)
  waiting for transfers between devices: 13.9 us -> 12.2 us
  Pallas kernels: 38.9 us -> 39.7 us
    all_to_all x1, waiting for transfers between devices: 6.34 us -> 4.66 us  [local(): lax.all_to_all(sent, ('wave', 'lev'), split_axis=0, concat_axis=0, tiled=...]
    pallas_call x3, Pallas kernels: 38 us -> 38.8 us  [the longest x1 13.3 us: legendre_sums(): pl.pallas_call(legendre_kernel, out_shape=[out, out, jax.ShapeDtypeStruct...]
  transfers between devices with their start and end apart: 3 -> 3, of which waited for: 3 -> 3; matrix products, arithmetic and copies ran while one was open for 0% -> 0% of each run, Pallas kernels for 15% -> 18%
where the time goes in v1:
time: 72.9 us; the launch traced here: 72.6 us
  Pallas kernels  39.7 us (54%)
  starting transfers between devices  18.6 us (26%)
  waiting for transfers between devices  12.2 us (17%)
  other arithmetic  0.83 us (1%)
  between operations  0.78 us (1%)
    all_to_all x1, starting transfers between devices, local(): lax.all_to_all(sent, ('wave', 'lev'), split_axis=0, concat_axis=0, tiled=...  14 us
    pallas_call x1, Pallas kernels, legendre_sums(): pl.pallas_call(legendre_kernel, out_shape=[out, out, jax.ShapeDtypeStruct...  13.3 us
    pallas_call x1, Pallas kernels, tables(): pl.pallas_call(table_kernel, out_shape=[table, table, jax.ShapeDtypeStruc...  12.9 us
    pallas_call x1, Pallas kernels, synthesis(): pl.pallas_call(synth_kernel, out_shape=jax.ShapeDtypeStruct((plev, 2, ROW...  12.6 us
    all_to_all x1, waiting for transfers between devices, local(): lax.all_to_all(energy, 'lev', split_axis=0, concat_axis=0, tiled=True)  4.82 us
    all_to_all x1, waiting for transfers between devices, local(): lax.all_to_all(sent, ('wave', 'lev'), split_axis=0, concat_axis=0, tiled=...  4.66 us
    all_to_all x1, starting transfers between devices, local(): lax.all_to_all(energy, 'lev', split_axis=0, concat_axis=0, tiled=True)  3.36 us
    ppermute x1, waiting for transfers between devices, local(): lax.ppermute(theirs, 'lev', pairs)  2.69 us
  transfers between devices with their start and end apart: 3, of which 3 were waited for; matrix products, arithmetic and copies ran while one was open for 0% of the time, Pallas kernels for 18%

profile of v1, /device:TPU:0, one launch (start us, length us, event | category | flops | bytes accessed | tf_op | source)
XLA Modules:
  0.0 72.6 jit_solution(225127816123203770)
XLA Ops:
  0.0 0.0 copy-start
  0.0 0.0 copy-start.1
  0.0 0.0 copy-start.2
  0.0 13.3 %legendre_sums.1 = (f32[32,40,128]{2,1,0:T(8,128)S(1)}, f32[32,40,128]{2,1,0:T(8,128)S(1)}, s32[1]{0:T(128)}) custom-call(s32[4]{0:T(128)} %brackets.1, f32[4]{0:T(128)} %weight_ref.1, s32[10,128]{1,0:T(8,128)} %bitcast.8, bf16[160,64,1280]{2,1,0:T(8,128)(2,1)} %spec_hbm.1, bf16[160,32,1280]{2,1,0:T(8,128)(2,1)} %leg_hbm.1), custom_call_target="tpu_custom_call" | custom-call | flops 1258291200 | bytes 32768000 | tf_op jit(solution)/shard_map/legendre_sums/pallas_call | solution.py:176
  13.3 0.0 copy-start.4
  13.3 0.0 copy-start.3
  14.0 4.9 %conditional.1 = (f32[32,40,128]{2,1,0:T(8,128)}) conditional(s32[]{:T(128)} %bitcast.1, (f32[32,40,128]{2,1,0:T(8,128)S(1)}, f32[32,40,128]{2,1,0:T(8,128)S(1)}) %tuple.12, (f32[32,40,128]{2,1,0:T(8,128)S(1)}, f32[32,40,128]{2,1,0:T(8,128)S(1)}) %tuple.12), branch_computations={%region_0.0_spmd, %region_1.0_spmd} | conditional | bytes 2621488 | solution.py:512
  14.1 1.3 %collective-permute-start.1 = (f32[32,40,128]{2,1,0:T(8,128)S(1)}, f32[32,40,128]{2,1,0:T(8,128)S(1)}, u32[]{:S(2)}, u32[]{:S(2)}) collective-permute-start(f32[32,40,128]{2,1,0:T(8,128)S(1)} %get-tuple-element.19), channel_id=1, source_target_pairs={{1,0},{2,1},{3,2},{5,4},{6,5},{7,6},{9,8},{10,9},{11,10},{13,12},{... | collective-permute-start | bytes 1966088 | tf_op jit(solution)/shard_map/cond/branch_1_fun/ppermute | solution.py:514
  15.4 2.7 %collective-permute-done.1.refs_1_ = f32[32,40,128]{2,1,0:T(8,128)S(1)} collective-permute-done((f32[32,40,128]{2,1,0:T(8,128)S(1)}, f32[32,40,128]{2,1,0:T(8,128)S(1)}, u32[]{:S(2)}, u32[]{:S(2)}) %collective-permute-start.1) | collective-permute-done | bytes 655392 | tf_op jit(solution)/shard_map/cond/branch_1_fun/ppermute | solution.py:514
  18.1 0.9 %join.3 = f32[32,40,128]{2,1,0:T(8,128)} custom-call(f32[32,40,128]{2,1,0:T(8,128)S(1)} %get-tuple-element.18.refs_0_, f32[32,40,128]{2,1,0:T(8,128)S(1)} %collective-permute-done.1.refs_1_), custom_call_target="tpu_custom_call" | custom-call | tf_op jit(solution)/shard_map/cond/branch_1_fun/join/pallas_call | solution.py:492
  19.0 14.0 %all-to-all-start = ((f32[32,40,128]{2,1,0:T(8,128)}), f32[32,40,128]{2,1,0:T(8,128)S(1)}, u32[]{:S(2)}, u32[]{:S(2)}) async-start(f32[32,40,128]{2,1,0:T(8,128)} %get-tuple-element.34), calls=%async_computation | async-start | bytes 1310720 | tf_op jit(solution)/shard_map/all_to_all | solution.py:519
  32.9 12.9 %fourier_tables.1 = (bf16[2,672,2560]{2,1,0:T(8,128)(2,1)}, bf16[2,672,2560]{2,1,0:T(8,128)(2,1)}, s32[8,160]{1,0:T(8,128)S(1)}) custom-call(s32[32]{0:T(128)} %points_ref.2, s32[10,128]{1,0:T(8,128)} %bitcast.9), custom_call_target="tpu_custom_call" | custom-call | flops 41287680 | bytes 13762560 | tf_op jit(solution)/shard_map/fourier_tables/pallas_call | solution.py:274
  45.8 0.1 reshape.53
  45.9 0.1 reshape.54.refs_1_
  46.0 4.7 %all-to-all-done = f32[32,40,128]{2,1,0:T(8,128)S(1)} async-done(((f32[32,40,128]{2,1,0:T(8,128)}), f32[32,40,128]{2,1,0:T(8,128)S(1)}, u32[]{:S(2)}, u32[]{:S(2)}) %all-to-all-start) | async-done | bytes 655392 | tf_op jit(solution)/shard_map/all_to_all | solution.py:519
  50.7 0.0 copy-done
  50.7 0.0 copy-done.1
  50.7 0.0 copy-done.2
  50.7 12.6 %synthesis.1 = f32[4,2,5248]{2,1,0:T(2,128)} custom-call(s32[32]{0:T(128)} %points_ref.2, f32[8,4,40,128]{3,2,1,0:T(8,128)S(1)} %bitcast.6, s32[1,1280]{1,0:T(1,128)S(1)} %reshape.54.refs_1_, bf16[2,4,256,256]{3,2,1,0:T(8,128)(2,1)S(1)} %copy-done, bf16[32,256]{1,0:T(8,128)(2,1)S(1)} %copy-done.2, bf16[256,256]{1,0:T(8,128)(2,1)S(1)} %copy-done.1, ...), custom_call_target="tpu_custom_call" | custom-call | flops 2642411520 | bytes 17039360 | tf_op jit(solution)/shard_map/synthesis/pallas_call | solution.py:453
  63.3 3.4 %all-to-all-start.1 = ((f32[4,2,5248]{2,1,0:T(2,128)}), f32[4,2,5248]{2,1,0:T(2,128)S(1)}, u32[]{:S(2)}, u32[]{:S(2)}) async-start(f32[4,2,5248]{2,1,0:T(2,128)} %synthesis.1), calls=%async_computation.1 | async-start | bytes 335872 | tf_op jit(solution)/shard_map/all_to_all | solution.py:525
  66.7 0.0 copy-done.4
  66.7 0.1 pad_add_fusion
  66.8 0.1 dynamic_slice.3
  66.9 4.8 %all-to-all-done.1 = f32[4,2,5248]{2,1,0:T(2,128)S(1)} async-done(((f32[4,2,5248]{2,1,0:T(2,128)}), f32[4,2,5248]{2,1,0:T(2,128)S(1)}, u32[]{:S(2)}, u32[]{:S(2)}) %all-to-all-start.1) | async-done | bytes 167968 | tf_op jit(solution)/shard_map/all_to_all | solution.py:525
  71.7 0.1 reshape.55
  71.8 0.0 copy-done.3
  71.8 0.8 %subtract_select_fusion = f32[1,8,5248]{2,1,0:T(8,128)} fusion(f32[1,8,5248]{2,1,0:T(8,128)S(1)} %reshape.55, f32[1,8,5248]{2,1,0:T(8,128)S(1)} %copy-done.3, s32[8]{0:T(128)S(1)} %dynamic_slice.3), kind=kLoop, calls=%fused_computation | loop fusion | flops 125952 | bytes 503840 | tf_op jit(solution)/shard_map/jit(_where)/select_n | solution.py:532
  (1 shorter events, 0.0 us)
Async XLA Ops:
  0.0 50.7 %copy-start = (bf16[2,4,256,256]{3,2,1,0:T(8,128)(2,1)S(1)}, bf16[2,4,256,256]{3,2,1,0:T(8,128)(2,1)}, u32[]{:S(2)}) copy-start(bf16[2,4,256,256]{3,2,1,0:T(8,128)(2,1)} %constant.22.clone.refs_2_) | copy-start | bytes 3145732
  0.0 50.7 %copy-start.1 = (bf16[256,256]{1,0:T(8,128)(2,1)S(1)}, bf16[256,256]{1,0:T(8,128)(2,1)}, u32[]{:S(2)}) copy-start(bf16[256,256]{1,0:T(8,128)(2,1)} %constant.24.clone.refs_4_) | copy-start | bytes 393220
  0.0 50.7 %copy-start.2 = (bf16[32,256]{1,0:T(8,128)(2,1)S(1)}, bf16[32,256]{1,0:T(8,128)(2,1)}, u32[]{:S(2)}) copy-start(bf16[32,256]{1,0:T(8,128)(2,1)} %constant.23.clone.refs_3_) | copy-start | bytes 49156
  13.3 53.4 %copy-start.4 = (s32[32]{0:T(128)S(1)}, s32[32]{0:T(128)}, u32[]{:S(2)}) copy-start(s32[32]{0:T(128)} %points_ref.2) | copy-start | bytes 388
  13.3 58.5 %copy-start.3 = (f32[1,8,5248]{2,1,0:T(8,128)S(1)}, f32[1,8,5248]{2,1,0:T(8,128)}, u32[]{:S(2)}) copy-start(f32[1,8,5248]{2,1,0:T(8,128)} %param.18) | copy-start | bytes 503812
  14.1 4.0 %collective-permute-start.1 = (f32[32,40,128]{2,1,0:T(8,128)S(1)}, f32[32,40,128]{2,1,0:T(8,128)S(1)}, u32[]{:S(2)}, u32[]{:S(2)}) collective-permute-start(f32[32,40,128]{2,1,0:T(8,128)S(1)} %get-tuple-element.19), channel_id=1, source_target_pairs={{1,0},{2,1},{3,2},{5,4},{6,5},{7,6},{9,8},{10,9},{11,10},{13,12},{... | collective-permute-start | bytes 1966088 | tf_op jit(solution)/shard_map/cond/branch_1_fun/ppermute | solution.py:514
  19.0 31.7 %all-to-all-start = ((f32[32,40,128]{2,1,0:T(8,128)}), f32[32,40,128]{2,1,0:T(8,128)S(1)}, u32[]{:S(2)}, u32[]{:S(2)}) async-start(f32[32,40,128]{2,1,0:T(8,128)} %get-tuple-element.34), calls=%async_computation | async-start | bytes 1310720 | tf_op jit(solution)/shard_map/all_to_all | solution.py:519
  63.3 8.4 %all-to-all-start.1 = ((f32[4,2,5248]{2,1,0:T(2,128)}), f32[4,2,5248]{2,1,0:T(2,128)S(1)}, u32[]{:S(2)}, u32[]{:S(2)}) async-start(f32[4,2,5248]{2,1,0:T(2,128)} %synthesis.1), calls=%async_computation.1 | async-start | bytes 335872 | tf_op jit(solution)/shard_map/all_to_all | solution.py:525
